TPU v7x, 256 devices: a whole 4x4x8 slice. The times are simulated.
256 devices in a mesh: dom: 16 (over z, y_lo), near: 16 (over y_hi, x, core).
Axes of the slice: x: 4, y: 4 (y_hi: 2, y_lo: 2; y = y_hi * 2 + y_lo), z: 8, core: 2. Of those that a mesh axis runs over, the one named last changes fastest.
Arguments:
- solution: float32 [56, 9, 32768], P(None, None, ('dom', 'near')), may hold values from -6 to 6
- star_matrices: float32 [3, 9, 9, 32768], P(None, None, None, ('dom', 'near')), may hold values from -2.5 to 2.5
- flux_plus: float32 [4, 9, 9, 32768], P(None, None, None, ('dom', 'near')), may hold values from -1.2 to 1.2
- flux_minus: float32 [4, 9, 9, 32768], P(None, None, None, ('dom', 'near')), may hold values from -1.2 to 1.2
- stiffness: float32 [3, 56, 56], replicated, may hold values from -0.75 to 0.75
- face_lift: float32 [4, 56, 21], replicated, may hold values from -0.625 to 0.625
- face_project: float32 [4, 21, 56], replicated, may hold values from -0.75 to 0.75
- cluster: int32 [32768], P(('dom', 'near')), may hold values from 0 to 1, as said below
- neighbour_part: int32 [4, 32768], P(None, ('dom', 'near')), may hold values from 0 to 4, as said below
- neighbour_slot: int32 [4, 32768], P(None, ('dom', 'near')), may hold values from 0 to 127, as said below
- neighbour_face: int32 [4, 32768], P(None, ('dom', 'near')), may hold values from 0 to 3
- orientation: int32 [4, 32768], P(None, ('dom', 'near')), may hold values from 0 to 2
- halo_send: int32 [4, 4096], P(None, ('dom', 'near')), may hold values from 0 to 127, as said below
Outputs:
- updated: float32 [56, 9, 32768], P(None, None, ('dom', 'near'))
Inputs may be any that keep to these rules, and one draw needn't show every extreme that they name: 0 marks an element that takes two half steps, 1 one that takes one step of length one. A partition holds at most 64 elements of cluster 0, and some partition exactly that many. `neighbour_part`: 0: the neighbour lies in the element's own partition; 1 to 4: it comes from the partition at near -1, near +1, dom -1, dom +1 (cyclic). In each partition each pair of a part p of 1 to 4 and a slot below 16 is named by exactly one face. `neighbour_slot`: an element of the own partition where the part is 0, a slot below 16 otherwise. `halo_send`: row r of a partition lists the elements it sends to the partition at near +1, near -1, dom +1, dom -1 for r = 0, 1, 2, 3; the 16 entries of a row are distinct.
All inputs are finite; a program needn't handle non-finite values.
Results may differ from a plain program's by a relative error of at most 0.0003.
Values sent between devices are 32-bit elements; how exact they have to be, the bound alone decides.
A program may use at most 128 MiB of HBM per device.

v0:
```python
import functools
import math

import jax
import jax.numpy as jnp
from jax import lax
from jax.experimental import pallas as pl
from jax.experimental.pallas import tpu as pltpu
from jax.sharding import PartitionSpec as P

MESH = pl.DeviceIdType.MESH
MODES = 56
FIELDS = 9
FACE_MODES = 21
ORDER = 6
E = 128
HALO = 16
KPAD = 64
FACE_PAD = 24
FACES = 4 * FACE_PAD
COLS = FIELDS * E
GROUPS = ((0, 1), (2, 3), (4, 5), (6, 7), (8,))
BF = jnp.bfloat16
F32 = jnp.float32


def orbit_nodes():
    degree = ORDER - 1
    nodes = [(a, b, degree - a - b) for a in range(degree + 1) for b in range(degree + 1 - a)]
    number = {node: n for n, node in enumerate(nodes)}
    seen, orbits = set(), []
    for node in nodes:
        if node in seen:
            continue
        a, b, c = node
        orbit = [(a, b, c), (b, c, a), (c, a, b)]
        seen.update(orbit)
        orbits.append([number[member] for member in orbit])
    order = [-1] * FACE_PAD
    for o, orbit in enumerate(orbits):
        for c in range(3):
            order[c * 8 + o] = orbit[c]
    return order


ORDERED = orbit_nodes()


def weights(begin, end):
    return [
        (end ** (k + 1) - begin ** (k + 1)) / math.factorial(k + 1) for k in range(ORDER)
    ]


def dot(a, b):
    return jnp.dot(a, b, preferred_element_type=F32)


def iota(shape, dim):
    return lax.broadcasted_iota(jnp.int32, shape, dim)


def ones_where(condition):
    return jnp.where(condition, 1.0, 0.0).astype(F32)


def high_low(x):
    high = x.astype(BF).astype(F32)
    return high, x - high


def place(x, marks):
    high, rest = high_low(x)
    middle, low = high_low(rest)
    marks = marks.astype(BF)
    return dot(high.astype(BF), marks) + dot(middle.astype(BF), marks) + dot(low.astype(BF), marks)


def place_left(marks, x):
    high, rest = high_low(x)
    middle, low = high_low(rest)
    marks = marks.astype(BF)
    return dot(marks, high.astype(BF)) + dot(marks, middle.astype(BF)) + dot(marks, low.astype(BF))


def threefold(matrix):
    high, low = high_low(matrix)
    row, col = iota((MODES, 3 * KPAD), 0), iota((MODES, 3 * KPAD), 1)
    twice = ones_where((col == row) | (col == row + KPAD)).astype(BF)
    last = ones_where(col == row + 2 * KPAD).astype(BF)
    return (dot(high.astype(BF), twice) + dot(low.astype(BF), last)).astype(BF)


def kernel(
    n_dom,
    n_near,
    sol_ref,
    star_ref,
    plus_ref,
    minus_ref,
    stiff_ref,
    lift_ref,
    proj_ref,
    cluster_ref,
    part_ref,
    slot_ref,
    nface_ref,
    turn_ref,
    halo_ref,
    out_ref,
    r_ref,
    y_ref,
    first_ref,
    second_ref,
    base_ref,
    x_ref,
    g_ref,
    prev_ref,
    a_ref,
    b_ref,
    p_ref,
    l_ref,
    ohl_ref,
    ohr_ref,
    ohs_ref,
    send_buf,
    recv_buf,
    send_sem,
    recv_sem,
):
    dom, near = lax.axis_index("dom"), lax.axis_index("near")
    targets = (
        (dom, lax.rem(near + 1, n_near)),
        (dom, lax.rem(near + n_near - 1, n_near)),
        (lax.rem(dom + 1, n_dom), near),
        (lax.rem(dom + n_dom - 1, n_dom), near),
    )
    barrier = pltpu.get_barrier_semaphore()
    for target in targets:
        pl.semaphore_signal(barrier, inc=1, device_id=target, device_id_type=MESH)

    def cols(f, count=1):
        return slice(f * E, (f + count) * E)

    stiff = jnp.concatenate([stiff_ref[d] for d in range(3)], axis=0)
    a_ref[...] = threefold(stiff)

    def split_into(t, f):
        high, low = high_low(t)
        zero = jnp.zeros((KPAD - MODES, E), F32)
        high = jnp.concatenate([high, zero], axis=0).astype(BF)
        low = jnp.concatenate([low, zero], axis=0).astype(BF)
        r_ref[0:KPAD, cols(f)] = high
        r_ref[KPAD : 2 * KPAD, cols(f)] = low
        r_ref[2 * KPAD : 3 * KPAD, cols(f)] = high

    def multiply(matrix, rows, group, slot):
        span = cols(group[0], len(group))
        y_ref[slot, 0:rows, span] = dot(matrix[...], r_ref[:, span])

    def star(group, slot, row0=0):
        totals = [None] * len(group)
        for d in range(3):
            for f in range(FIELDS):
                y = y_ref[slot, row0 + d * MODES : row0 + (d + 1) * MODES, cols(f)]
                for n, g in enumerate(group):
                    term = star_ref[f, g, d : d + 1, :] * y
                    totals[n] = term if totals[n] is None else totals[n] + term
        return totals

    half, rest = weights(0.0, 0.5), weights(0.5, 1.0)

    def pick(table, k):
        value = jnp.float32(table[0])
        for n in range(1, len(table)):
            value = jnp.where(k == n, jnp.float32(table[n]), value)
        return value

    small = cluster_ref[...] == 0

    for group in GROUPS:
        for f in group:
            u = sol_ref[f]
            split_into(u, f)
            first_ref[f] = half[0] * u
            second_ref[f] = rest[0] * u
        multiply(a_ref, 3 * MODES, group, 0)

    backward = jnp.concatenate([stiff_ref[d].T for d in range(3)], axis=0)
    node, entry = iota((FACE_PAD, FACE_MODES), 1), iota((FACE_PAD, FACE_MODES), 0)
    chosen = entry < 0
    for spot, number in enumerate(ORDERED):
        if number >= 0:
            chosen = chosen | ((entry == spot) & (node == number))
    chosen = ones_where(chosen)
    project = jnp.concatenate([place_left(chosen, proj_ref[:, j, :]) for j in range(4)], axis=0)
    lifts = jnp.concatenate([place_left(chosen, lift_ref[:, j, :]) for j in range(4)], axis=0)
    b_ref[...] = threefold(jnp.concatenate([project, backward], axis=0))
    p_ref[...] = threefold(project)
    lift_high, lift_low = high_low(lifts.T)
    row, col = iota((FACES, 2 * FACES), 0), iota((FACES, 2 * FACES), 1)
    twice = ones_where((col == row) | (col == row + FACES)).astype(BF)
    once = ones_where(col == row).astype(BF)
    l_ref[...] = jnp.concatenate(
        [dot(lift_high.astype(BF), twice), dot(lift_low.astype(BF), once)], axis=0
    ).astype(BF)

    part, slot_of = part_ref[...], slot_ref[...]
    face_of = nface_ref[...]
    local_key = jnp.where(part == 0, face_of * E + slot_of, -1)
    remote_key = jnp.where(part > 0, face_of * (4 * HALO) + (part - 1) * HALO + slot_of, -1)
    for i in range(4):
        ohl_ref[:, cols(i)] = ones_where(local_key[i : i + 1, :] == iota((4 * E, E), 0)).astype(BF)
        ohr_ref[:, cols(i)] = ones_where(
            remote_key[i : i + 1, :] == iota((16 * HALO, E), 0)
        ).astype(BF)
    spread = ones_where(iota((HALO, E), 0) == lax.rem(iota((HALO, E), 1), HALO)).astype(BF)
    sent = dot(halo_ref[...].astype(F32).astype(BF), spread)
    for r in range(4):
        ohs_ref[:, cols(r)] = ones_where(
            sent[r : r + 1, :] == iota((2 * E, E), 0).astype(F32)
        ).astype(BF) + ones_where(
            sent[r : r + 1, :] + float(E) == iota((2 * E, E), 0).astype(F32)
        ).astype(BF)

    lane = iota((1, E), 1)
    lane_group = lane // HALO

    def taylor_rest(first_only):
        def body(k, carry):
            old, new = lax.rem(k, 2), lax.rem(k + 1, 2)
            w1, w2 = pick(half, k + 1), pick(rest, k + 1)
            for group in GROUPS:
                for g, t in zip(group, star(group, old)):
                    split_into(t, g)
                    first_ref[g] += w1 * t
                    if not first_only:
                        second_ref[g] += w2 * t
                multiply(a_ref, 3 * MODES, group, new)
            return carry

        lax.fori_loop(0, ORDER - 2, body, 0)
        for group in GROUPS:
            for g, t in zip(group, star(group, 0)):
                value = first_ref[g] + half[5] * t
                if first_only:
                    value = jnp.where(small, value, second_ref[g])
                else:
                    second_ref[g] += rest[5] * t
                first_ref[g] = value

    def exchange(phase):
        copies = []
        highs, lows = [], []
        for f in range(FIELDS):
            high, low = high_low(first_ref[f])
            highs.append(high)
            lows.append(low)
        stacked = jnp.concatenate(
            [
                jnp.concatenate(highs, axis=0).astype(BF),
                jnp.concatenate(lows, axis=0).astype(BF),
            ],
            axis=1,
        )
        taken = dot(stacked, ohs_ref[...])
        for r in range(4):
            block = taken[:, cols(r)]
            packed = block[0:MODES]
            for f in range(1, 8):
                packed = jnp.where(lane_group == f, block[f * MODES : (f + 1) * MODES], packed)
            tail = block[8 * MODES : 8 * MODES + 8]
            for k in range(1, 7):
                start = 8 * MODES + 8 * k
                tail = jnp.where(lane_group == k, block[start : start + 8], tail)
            send_buf[phase, r] = jnp.concatenate([packed, tail], axis=0)
        if phase == 0:
            pl.semaphore_wait(barrier, 4)
        for r in range(4):
            copy = pltpu.make_async_remote_copy(
                src_ref=send_buf.at[phase, r],
                dst_ref=recv_buf.at[phase, r],
                send_sem=send_sem.at[phase, r],
                recv_sem=recv_sem.at[phase, r],
                device_id=targets[r],
                device_id_type=MESH,
            )
            copy.start()
            copies.append(copy)
        return copies

    def gather(blocks, marks):
        sides = []
        for block in blocks:
            high, low = high_low(block)
            sides.append(jnp.concatenate([high, low], axis=0).astype(BF))
        both = dot(jnp.concatenate(sides, axis=1), marks[...])
        rows = FIELDS * FACE_PAD
        return both[0:rows] + both[rows : 2 * rows]

    def by_field(read):
        return jnp.concatenate([read(f) for f in range(FIELDS)], axis=0)

    def local_part():
        for group in GROUPS:
            for f in group:
                split_into(first_ref[f], f)
            multiply(b_ref, FACES + 3 * MODES, group, 0)
        g_ref[...] = gather(
            [
                by_field(lambda f: y_ref[0, j * FACE_PAD : (j + 1) * FACE_PAD, cols(f)])
                for j in range(4)
            ],
            ohl_ref,
        )
        for i in range(4):
            totals = [None] * FIELDS
            for f in range(FIELDS):
                y = y_ref[0, i * FACE_PAD : (i + 1) * FACE_PAD, cols(f)]
                for g in range(FIELDS):
                    term = plus_ref[f, g, i : i + 1, :] * y
                    totals[g] = term if totals[g] is None else totals[g] + term
            for g in range(FIELDS):
                x_ref[i * FACE_PAD : (i + 1) * FACE_PAD, cols(g)] = totals[g]
        for group in GROUPS:
            for g, v in zip(group, star(group, 0, FACES)):
                base_ref[g] += v

    def remote_part(phase, copies):
        for copy in copies:
            copy.wait()
        rolled = []
        for r in range(4):
            block = recv_buf[phase, r]
            rolled.append(
                [block if c == 0 else pltpu.roll(block, c * HALO, 1) for c in range(8)]
            )

        def collect(at, rows):
            value = None
            for spot in range(8):
                r = spot % 4
                piece = rolled[r][(spot - at) % 8][rows]
                value = piece if value is None else jnp.where(lane_group == spot, piece, value)
            return value

        for group in GROUPS:
            for f in group:
                if f < 8:
                    split_into(collect(f, slice(0, MODES)), f)
                else:
                    tiles = [collect(k, slice(MODES, MODES + 8)) for k in range(7)]
                    split_into(jnp.concatenate(tiles, axis=0), f)
            multiply(p_ref, FACES, group, 1)

        def pair(j):
            def read(f):
                low = y_ref[1, j * FACE_PAD : (j + 1) * FACE_PAD, cols(f)]
                high = y_ref[1, (j + 1) * FACE_PAD : (j + 2) * FACE_PAD, cols(f)]
                return jnp.where(lane < E // 2, low, high)

            return by_field(read)

        g_ref[...] += gather([pair(0), pair(2)], ohr_ref)
        for i in range(4):
            turn = turn_ref[i : i + 1, :]
            for_one, for_two = turn == 1, turn == 2
            totals = [x_ref[i * FACE_PAD : (i + 1) * FACE_PAD, cols(g)] for g in range(FIELDS)]
            for f in range(FIELDS):
                raw = g_ref[f * FACE_PAD : (f + 1) * FACE_PAD, cols(i)]
                v = [raw[c * 8 : (c + 1) * 8] for c in range(3)]
                y = jnp.concatenate(
                    [
                        jnp.where(
                            for_one, v[(c + 1) % 3], jnp.where(for_two, v[(c + 2) % 3], v[c])
                        )
                        for c in range(3)
                    ],
                    axis=0,
                )
                for g in range(FIELDS):
                    totals[g] = totals[g] + minus_ref[f, g, i : i + 1, :] * y
            for g in range(FIELDS):
                x_ref[i * FACE_PAD : (i + 1) * FACE_PAD, cols(g)] = totals[g]

    def lifted(group):
        for g in group:
            high, low = high_low(x_ref[:, cols(g)])
            r_ref[0:FACES, cols(g)] = high.astype(BF)
            r_ref[FACES : 2 * FACES, cols(g)] = low.astype(BF)
        both = dot(l_ref[...], r_ref[:, cols(group[0], len(group))])
        return [
            both[0:MODES, cols(n)] + both[MODES : 2 * MODES, cols(n)] for n in range(len(group))
        ]

    taylor_rest(False)
    copies = exchange(0)
    for f in range(FIELDS):
        base_ref[f] = sol_ref[f]
    local_part()
    remote_part(0, copies)
    for group in GROUPS:
        update = lifted(group)
        for n, g in enumerate(group):
            stepped = base_ref[g] - update[n]
            base_ref[g] = stepped
            prev_ref[g] = jnp.where(small, stepped, sol_ref[g])
    for group in GROUPS:
        for f in group:
            u = prev_ref[f]
            split_into(u, f)
            first_ref[f] = half[0] * u
        multiply(a_ref, 3 * MODES, group, 0)
    taylor_rest(True)
    copies = exchange(1)
    local_part()
    remote_part(1, copies)
    for group in GROUPS:
        update = lifted(group)
        for n, g in enumerate(group):
            out_ref[g] = base_ref[g] - update[n]


def on_device(
    n_dom,
    n_near,
    solution,
    star_matrices,
    flux_plus,
    flux_minus,
    stiffness,
    face_lift,
    face_project,
    cluster,
    neighbour_part,
    neighbour_slot,
    neighbour_face,
    orientation,
    halo_send,
):
    field_block = pltpu.VMEM((FIELDS, MODES, E), F32)
    step = pl.pallas_call(
        functools.partial(kernel, n_dom, n_near),
        out_shape=jax.ShapeDtypeStruct((FIELDS, MODES, E), F32),
        in_specs=[pl.BlockSpec(memory_space=pltpu.VMEM)] * 13,
        out_specs=pl.BlockSpec(memory_space=pltpu.VMEM),
        scratch_shapes=[
            pltpu.VMEM((3 * KPAD, COLS), BF),
            pltpu.VMEM((2, FACES + 3 * MODES, COLS), F32),
            field_block,
            field_block,
            field_block,
            pltpu.VMEM((FACES, COLS), F32),
            pltpu.VMEM((FIELDS * FACE_PAD, 4 * E), F32),
            field_block,
            pltpu.VMEM((3 * MODES, 3 * KPAD), BF),
            pltpu.VMEM((FACES + 3 * MODES, 3 * KPAD), BF),
            pltpu.VMEM((FACES, 3 * KPAD), BF),
            pltpu.VMEM((2 * MODES, 2 * FACES), BF),
            pltpu.VMEM((4 * E, 4 * E), BF),
            pltpu.VMEM((16 * HALO, 4 * E), BF),
            pltpu.VMEM((2 * E, 4 * E), BF),
            pltpu.VMEM((2, 4, KPAD, E), F32),
            pltpu.VMEM((2, 4, KPAD, E), F32),
            pltpu.SemaphoreType.DMA((2, 4)),
            pltpu.SemaphoreType.DMA((2, 4)),
        ],
        compiler_params=pltpu.CompilerParams(
            collective_id=0, has_side_effects=True, vmem_limit_bytes=40 * 2**20
        ),
        name="cluster_step",
    )
    out = step(
        jnp.transpose(solution, (1, 0, 2)),
        jnp.transpose(star_matrices, (1, 2, 0, 3)),
        jnp.transpose(flux_plus, (1, 2, 0, 3)),
        jnp.transpose(flux_minus, (1, 2, 0, 3)),
        stiffness,
        jnp.transpose(face_lift, (2, 0, 1)),
        jnp.transpose(face_project, (1, 0, 2)),
        cluster.reshape(1, E),
        neighbour_part,
        neighbour_slot,
        neighbour_face,
        orientation,
        halo_send,
    )
    return jnp.transpose(out, (1, 0, 2))


def solution(mesh):
    both = ("dom", "near")
    in_specs = (
        P(None, None, both),
        P(None, None, None, both),
        P(None, None, None, both),
        P(None, None, None, both),
        P(),
        P(),
        P(),
        P(both),
        P(None, both),
        P(None, both),
        P(None, both),
        P(None, both),
        P(None, both),
    )
    return jax.shard_map(
        functools.partial(on_device, mesh.shape["dom"], mesh.shape["near"]),
        mesh=mesh,
        in_specs=in_specs,
        out_specs=P(None, None, both),
        check_vma=False,
    )
```

profile of v0, /device:TPU:7, one launch (start us, length us, event | category | flops | bytes accessed | tf_op | source)
XLA Modules:
  0.0 39.0 jit_solution(11804568641793489242)
XLA Ops:
  0.0 0.0 copy-start.11
  0.0 0.0 copy-start.10
  0.0 0.0 copy-start.9
  0.0 0.0 copy-start.8
  0.0 0.0 copy-start.7
  0.0 0.0 copy-start.12
  0.0 0.6 %copy-done.11 = s32[4,16]{1,0:T(4,128)S(1)} copy-done((s32[4,16]{1,0:T(4,128)S(1)}, s32[4,16]{1,0:T(4,128)}, u32[]{:S(2)}) %copy-start.11) | copy-done | bytes 280
  0.7 0.0 copy-done.10
  0.7 0.0 copy-done.9
  0.7 0.0 copy-done.8
  0.7 0.0 copy-done.7
  0.7 0.0 copy-done.12
  0.7 0.0 copy-start
  0.8 0.9 %copy-done = f32[56,9,128]{2,0,1:T(8,128)S(1)} copy-done((f32[56,9,128]{2,0,1:T(8,128)S(1)}, f32[56,9,128]{2,0,1:T(8,128)}, u32[]{:S(2)}) %copy-start) | copy-done | bytes 258072
  1.7 0.0 copy-start.1
  1.7 0.9 %copy-done.1 = f32[3,9,9,128]{3,0,2,1:T(4,128)S(1)} copy-done((f32[3,9,9,128]{3,0,2,1:T(4,128)S(1)}, f32[3,9,9,128]{3,0,2,1:T(4,128)}, u32[]{:S(2)}) %copy-start.1) | copy-done | bytes 124440
  2.6 0.0 copy-start.2
  2.6 0.9 %copy-done.2 = f32[4,9,9,128]{3,0,2,1:T(4,128)S(1)} copy-done((f32[4,9,9,128]{3,0,2,1:T(4,128)S(1)}, f32[4,9,9,128]{3,0,2,1:T(4,128)}, u32[]{:S(2)}) %copy-start.2) | copy-done | bytes 165912
  3.5 0.0 copy-start.3
  3.5 0.9 %copy-done.3 = f32[4,9,9,128]{3,0,2,1:T(4,128)S(1)} copy-done((f32[4,9,9,128]{3,0,2,1:T(4,128)S(1)}, f32[4,9,9,128]{3,0,2,1:T(4,128)}, u32[]{:S(2)}) %copy-start.3) | copy-done | bytes 165912
  4.4 0.0 copy-start.4
  4.5 0.9 %copy-done.4 = f32[3,56,56]{2,1,0:T(8,128)S(1)} copy-done((f32[3,56,56]{2,1,0:T(8,128)S(1)}, f32[3,56,56]{2,1,0:T(8,128)}, u32[]{:S(2)}) %copy-start.4) | copy-done | bytes 37656
  5.3 0.0 copy-start.5
  5.3 0.8 %copy-done.5 = f32[4,56,21]{1,0,2:T(4,128)S(1)} copy-done((f32[4,56,21]{1,0,2:T(4,128)S(1)}, f32[4,56,21]{1,0,2:T(4,128)}, u32[]{:S(2)}) %copy-start.5) | copy-done | bytes 18840
  6.1 0.0 copy-start.6
  6.1 0.8 %copy-done.6 = f32[4,21,56]{2,0,1:T(4,128)S(1)} copy-done((f32[4,21,56]{2,0,1:T(4,128)S(1)}, f32[4,21,56]{2,0,1:T(4,128)}, u32[]{:S(2)}) %copy-start.6) | copy-done | bytes 18840
  6.9 31.4 %cluster_step.1 = f32[9,56,128]{2,1,0:T(8,128)S(1)} custom-call(f32[9,56,128]{2,1,0:T(8,128)S(1)} %bitcast.9, f32[9,9,3,128]{3,2,1,0:T(4,128)S(1)} %bitcast.10, f32[9,9,4,128]{3,2,1,0:T(4,128)S(1)} %bitcast.11, f32[9,9,4,128]{3,2,1,0:T(4,128)S(1)} %bitcast.12, f32[3,56,56]{2,1,0:T(8,128)S(1)} %copy-done.4, f32[21,4,56]{2,1,0:T(4,128)S(1)} %bitcast.13, ...), custom_call_target="tpu_custom_call" | custom-call | tf_op jit(solution)/shard_map/cluster_step/pallas_call | solution.py:473
  38.3 0.7 %copy.15 = f32[56,9,128]{2,0,1:T(8,128)} copy(f32[56,9,128]{2,0,1:T(8,128)S(1)} %bitcast.8) | data formatting | bytes 516096
Async XLA Ops:
  0.0 0.7 %copy-start.11 = (s32[4,16]{1,0:T(4,128)S(1)}, s32[4,16]{1,0:T(4,128)}, u32[]{:S(2)}) copy-start(s32[4,16]{1,0:T(4,128)} %halo_ref.1) | copy-start | bytes 772
  0.0 0.7 %copy-start.10 = (s32[4,128]{1,0:T(4,128)S(1)}, s32[4,128]{1,0:T(4,128)}, u32[]{:S(2)}) copy-start(s32[4,128]{1,0:T(4,128)} %turn_ref.1) | copy-start | bytes 6148
  0.0 0.7 %copy-start.9 = (s32[4,128]{1,0:T(4,128)S(1)}, s32[4,128]{1,0:T(4,128)}, u32[]{:S(2)}) copy-start(s32[4,128]{1,0:T(4,128)} %nface_ref.1) | copy-start | bytes 6148
  0.0 0.7 %copy-start.8 = (s32[4,128]{1,0:T(4,128)S(1)}, s32[4,128]{1,0:T(4,128)}, u32[]{:S(2)}) copy-start(s32[4,128]{1,0:T(4,128)} %slot_ref.1) | copy-start | bytes 6148
  0.0 0.7 %copy-start.7 = (s32[4,128]{1,0:T(4,128)S(1)}, s32[4,128]{1,0:T(4,128)}, u32[]{:S(2)}) copy-start(s32[4,128]{1,0:T(4,128)} %part_ref.1) | copy-start | bytes 6148
  0.0 0.7 %copy-start.12 = (s32[128]{0:T(128)S(1)}, s32[128]{0:T(128)}, u32[]{:S(2)}) copy-start(s32[128]{0:T(128)} %param.20) | copy-start | bytes 1540
  0.7 0.9 %copy-start = (f32[56,9,128]{2,0,1:T(8,128)S(1)}, f32[56,9,128]{2,0,1:T(8,128)}, u32[]{:S(2)}) copy-start(f32[56,9,128]{2,0,1:T(8,128)} %param.13) | copy-start | bytes 774148
  1.7 0.9 %copy-start.1 = (f32[3,9,9,128]{3,0,2,1:T(4,128)S(1)}, f32[3,9,9,128]{3,0,2,1:T(4,128)}, u32[]{:S(2)}) copy-start(f32[3,9,9,128]{3,0,2,1:T(4,128)} %param.14) | copy-start | bytes 373252
  2.6 0.9 %copy-start.2 = (f32[4,9,9,128]{3,0,2,1:T(4,128)S(1)}, f32[4,9,9,128]{3,0,2,1:T(4,128)}, u32[]{:S(2)}) copy-start(f32[4,9,9,128]{3,0,2,1:T(4,128)} %param.15) | copy-start | bytes 497668
  3.5 0.9 %copy-start.3 = (f32[4,9,9,128]{3,0,2,1:T(4,128)S(1)}, f32[4,9,9,128]{3,0,2,1:T(4,128)}, u32[]{:S(2)}) copy-start(f32[4,9,9,128]{3,0,2,1:T(4,128)} %param.16) | copy-start | bytes 497668
  4.4 0.9 %copy-start.4 = (f32[3,56,56]{2,1,0:T(8,128)S(1)}, f32[3,56,56]{2,1,0:T(8,128)}, u32[]{:S(2)}) copy-start(f32[3,56,56]{2,1,0:T(8,128)} %stiff_ref.1) | copy-start | bytes 112900
  5.3 0.8 %copy-start.5 = (f32[4,56,21]{1,0,2:T(4,128)S(1)}, f32[4,56,21]{1,0,2:T(4,128)}, u32[]{:S(2)}) copy-start(f32[4,56,21]{1,0,2:T(4,128)} %param.18) | copy-start | bytes 56452
  6.1 0.8 %copy-start.6 = (f32[4,21,56]{2,0,1:T(4,128)S(1)}, f32[4,21,56]{2,0,1:T(4,128)}, u32[]{:S(2)}) copy-start(f32[4,21,56]{2,0,1:T(4,128)} %param.19) | copy-start | bytes 56452
where the time goes:
time: 39.4 us; the launch traced here: 39 us
  Pallas kernels  31.4 us (80%)
  local copies, waits for them, and re-layouts  7.57 us (19%)
    pallas_call x1, Pallas kernels, on_device(): step(jnp.transpose(solution, (1, 0, 2)), jnp.transpose(star_matrices, (1,...  31.4 us
    unnamed x27, local copies, waits for them, and re-layouts  7.57 us

commit v1 on v0

--- a/solution.py
+++ b/solution.py
@@ -94,40 +94,52 @@
 def kernel(
     n_dom,
     n_near,
-    sol_ref,
-    star_ref,
-    plus_ref,
-    minus_ref,
-    stiff_ref,
-    lift_ref,
-    proj_ref,
-    cluster_ref,
-    part_ref,
-    slot_ref,
-    nface_ref,
-    turn_ref,
-    halo_ref,
-    out_ref,
-    r_ref,
-    y_ref,
-    first_ref,
-    second_ref,
-    base_ref,
-    x_ref,
-    g_ref,
-    prev_ref,
-    a_ref,
-    b_ref,
-    p_ref,
-    l_ref,
-    ohl_ref,
-    ohr_ref,
-    ohs_ref,
-    send_buf,
-    recv_buf,
-    send_sem,
-    recv_sem,
+    *refs,
 ):
+    sources, out_ref, held = refs[:13], refs[13], refs[14:27]
+    (
+        sol_ref,
+        star_ref,
+        plus_ref,
+        minus_ref,
+        stiff_ref,
+        lift_ref,
+        proj_ref,
+        cluster_ref,
+        part_ref,
+        slot_ref,
+        nface_ref,
+        turn_ref,
+        halo_ref,
+    ) = held
+    (
+        r_ref,
+        y_ref,
+        first_ref,
+        second_ref,
+        base_ref,
+        x_ref,
+        g_ref,
+        prev_ref,
+        a_ref,
+        b_ref,
+        p_ref,
+        l_ref,
+        ohl_ref,
+        ohr_ref,
+        ohs_ref,
+        send_buf,
+        recv_buf,
+        send_sem,
+        recv_sem,
+        load_sem,
+    ) = refs[27:]
+    loads = [
+        pltpu.make_async_copy(source, target, load_sem.at[n])
+        for n, (source, target) in enumerate(zip(sources, held))
+    ]
+    for n in (4, 0, 1, 12, 7, 8, 9, 10, 5, 6, 2, 3, 11):
+        loads[n].start()
     dom, near = lax.axis_index("dom"), lax.axis_index("near")
     targets = (
         (dom, lax.rem(near + 1, n_near)),
@@ -142,6 +154,7 @@
     def cols(f, count=1):
         return slice(f * E, (f + count) * E)
 
+    loads[4].wait()
     stiff = jnp.concatenate([stiff_ref[d] for d in range(3)], axis=0)
     a_ref[...] = threefold(stiff)
 
@@ -170,14 +183,7 @@
 
     half, rest = weights(0.0, 0.5), weights(0.5, 1.0)
 
-    def pick(table, k):
-        value = jnp.float32(table[0])
-        for n in range(1, len(table)):
-            value = jnp.where(k == n, jnp.float32(table[n]), value)
-        return value
-
-    small = cluster_ref[...] == 0
-
+    loads[0].wait()
     for group in GROUPS:
         for f in group:
             u = sol_ref[f]
@@ -186,6 +192,9 @@
             second_ref[f] = rest[0] * u
         multiply(a_ref, 3 * MODES, group, 0)
 
+    for n in (1, 12, 7, 8, 9, 10, 5, 6):
+        loads[n].wait()
+    small = cluster_ref[...] == 0
     backward = jnp.concatenate([stiff_ref[d].T for d in range(3)], axis=0)
     node, entry = iota((FACE_PAD, FACE_MODES), 1), iota((FACE_PAD, FACE_MODES), 0)
     chosen = entry < 0
@@ -227,19 +236,14 @@
     lane_group = lane // HALO
 
     def taylor_rest(first_only):
-        def body(k, carry):
-            old, new = lax.rem(k, 2), lax.rem(k + 1, 2)
-            w1, w2 = pick(half, k + 1), pick(rest, k + 1)
+        for k in range(ORDER - 2):
             for group in GROUPS:
-                for g, t in zip(group, star(group, old)):
+                for g, t in zip(group, star(group, k % 2)):
                     split_into(t, g)
-                    first_ref[g] += w1 * t
+                    first_ref[g] += half[k + 1] * t
                     if not first_only:
-                        second_ref[g] += w2 * t
-                multiply(a_ref, 3 * MODES, group, new)
-            return carry
-
-        lax.fori_loop(0, ORDER - 2, body, 0)
+                        second_ref[g] += rest[k + 1] * t
+                multiply(a_ref, 3 * MODES, group, (k + 1) % 2)
         for group in GROUPS:
             for g, t in zip(group, star(group, 0)):
                 value = first_ref[g] + half[5] * t
@@ -395,6 +399,8 @@
 
     taylor_rest(False)
     copies = exchange(0)
+    for n in (2, 3, 11):
+        loads[n].wait()
     for f in range(FIELDS):
         base_ref[f] = sol_ref[f]
     local_part()
@@ -438,13 +444,29 @@
     orientation,
     halo_send,
 ):
+    operands = (
+        jnp.transpose(solution, (1, 0, 2)),
+        jnp.transpose(star_matrices, (1, 2, 0, 3)),
+        jnp.transpose(flux_plus, (1, 2, 0, 3)),
+        jnp.transpose(flux_minus, (1, 2, 0, 3)),
+        stiffness,
+        jnp.transpose(face_lift, (2, 0, 1)),
+        jnp.transpose(face_project, (1, 0, 2)),
+        cluster.reshape(1, E),
+        neighbour_part,
+        neighbour_slot,
+        neighbour_face,
+        orientation,
+        halo_send,
+    )
     field_block = pltpu.VMEM((FIELDS, MODES, E), F32)
     step = pl.pallas_call(
         functools.partial(kernel, n_dom, n_near),
         out_shape=jax.ShapeDtypeStruct((FIELDS, MODES, E), F32),
-        in_specs=[pl.BlockSpec(memory_space=pltpu.VMEM)] * 13,
+        in_specs=[pl.BlockSpec(memory_space=pltpu.HBM)] * 13,
         out_specs=pl.BlockSpec(memory_space=pltpu.VMEM),
-        scratch_shapes=[
+        scratch_shapes=[pltpu.VMEM(value.shape, value.dtype) for value in operands]
+        + [
             pltpu.VMEM((3 * KPAD, COLS), BF),
             pltpu.VMEM((2, FACES + 3 * MODES, COLS), F32),
             field_block,
@@ -464,27 +486,14 @@
             pltpu.VMEM((2, 4, KPAD, E), F32),
             pltpu.SemaphoreType.DMA((2, 4)),
             pltpu.SemaphoreType.DMA((2, 4)),
+            pltpu.SemaphoreType.DMA((13,)),
         ],
         compiler_params=pltpu.CompilerParams(
-            collective_id=0, has_side_effects=True, vmem_limit_bytes=40 * 2**20
+            collective_id=0, has_side_effects=True, vmem_limit_bytes=60 * 2**20
         ),
         name="cluster_step",
     )
-    out = step(
-        jnp.transpose(solution, (1, 0, 2)),
-        jnp.transpose(star_matrices, (1, 2, 0, 3)),
-        jnp.transpose(flux_plus, (1, 2, 0, 3)),
-        jnp.transpose(flux_minus, (1, 2, 0, 3)),
-        stiffness,
-        jnp.transpose(face_lift, (2, 0, 1)),
-        jnp.transpose(face_project, (1, 0, 2)),
-        cluster.reshape(1, E),
-        neighbour_part,
-        neighbour_slot,
-        neighbour_face,
-        orientation,
-        halo_send,
-    )
+    out = step(*operands)
     return jnp.transpose(out, (1, 0, 2))
 
 

time: 39.4 us -> 29.1 us (0.74)
  local copies, waits for them, and re-layouts: 7.57 us -> 1.66 us
  Pallas kernels: 31.4 us -> 27.3 us
    unnamed x27 -> x1, local copies, waits for them, and re-layouts: 7.57 us -> 1.66 us
    pallas_call x1, Pallas kernels: 31.4 us -> 27.3 us  [on_device(): out = step(*operands)]
where the time goes in v1:
time: 29.1 us; the launch traced here: 29 us
  Pallas kernels  27.3 us (94%)
  local copies, waits for them, and re-layouts  1.66 us (6%)
    pallas_call x1, Pallas kernels, on_device(): out = step(*operands)  27.3 us
    unnamed x1, local copies, waits for them, and re-layouts  1.66 us

profile of v1, /device:TPU:7, one launch (start us, length us, event | category | flops | bytes accessed | tf_op | source)
XLA Modules:
  0.0 29.0 jit_solution(4408979099247914769)
XLA Ops:
  0.0 27.3 %cluster_step.1 = f32[9,56,128]{2,1,0:T(8,128)} custom-call(f32[9,56,128]{2,1,0:T(8,128)} %bitcast.9, f32[9,9,3,128]{3,2,1,0:T(4,128)} %bitcast.10, f32[9,9,4,128]{3,2,1,0:T(4,128)} %bitcast.11, f32[9,9,4,128]{3,2,1,0:T(4,128)} %bitcast.12, f32[3,56,56]{2,1,0:T(8,128)} %refs_4_.1, f32[21,4,56]{2,1,0:T(4,128)} %bitcast.13, f32[21,4,56]{2,1,0:T(4,128)} %bitcast.14, ...), custom_call_target="tpu_custom_call" | custom-call | tf_op jit(solution)/shard_map/cluster_step/pallas_call | solution.py:496
  27.3 1.7 %copy.15 = f32[56,9,128]{2,0,1:T(8,128)} copy(f32[56,9,128]{2,0,1:T(8,128)} %bitcast.8) | data formatting | bytes 516096

commit v2 on v1

--- a/solution.py
+++ b/solution.py
@@ -15,6 +15,9 @@
 ORDER = 6
 E = 128
 HALO = 16
+PACK = 64
+PAIRS = ((0, 1), (2, 3), (4, 5), (6, 7), (8,))
+PAIR_GROUPS = ((0, 1), (2, 3), (4,))
 KPAD = 64
 FACE_PAD = 24
 FACES = 4 * FACE_PAD
@@ -120,7 +123,6 @@
         base_ref,
         x_ref,
         g_ref,
-        prev_ref,
         a_ref,
         b_ref,
         p_ref,
@@ -133,6 +135,11 @@
         send_sem,
         recv_sem,
         load_sem,
+        star8_ref,
+        packed_star_ref,
+        compact_ref,
+        widen_ref,
+        j_ref,
     ) = refs[27:]
     loads = [
         pltpu.make_async_copy(source, target, load_sem.at[n])
@@ -171,13 +178,16 @@
         span = cols(group[0], len(group))
         y_ref[slot, 0:rows, span] = dot(matrix[...], r_ref[:, span])
 
+    def spread_mul(tile, y):
+        return (tile[None] * y.reshape(MODES // 8, 8, E)).reshape(MODES, E)
+
     def star(group, slot, row0=0):
         totals = [None] * len(group)
         for d in range(3):
             for f in range(FIELDS):
                 y = y_ref[slot, row0 + d * MODES : row0 + (d + 1) * MODES, cols(f)]
                 for n, g in enumerate(group):
-                    term = star_ref[f, g, d : d + 1, :] * y
+                    term = spread_mul(star8_ref[f, g, d], y)
                     totals[n] = term if totals[n] is None else totals[n] + term
         return totals
 
@@ -195,6 +205,25 @@
     for n in (1, 12, 7, 8, 9, 10, 5, 6):
         loads[n].wait()
     small = cluster_ref[...] == 0
+    for f in range(FIELDS):
+        for g in range(FIELDS):
+            for d in range(3):
+                star8_ref[f, g, d] = jnp.broadcast_to(star_ref[f, g, d : d + 1, :], (8, E))
+    before = ones_where(iota((E, E), 0) < iota((E, E), 1)).astype(BF)
+    small_row = ones_where(small)
+    rank_row = dot(jnp.broadcast_to(small_row, (8, E)).astype(BF), before)[0:1]
+    rank_row = jnp.where(small, rank_row, -1.0)
+    square = iota((E, E), 0) == iota((E, E), 1)
+    rank_col = jnp.sum(jnp.where(square, rank_row, 0.0), axis=1, keepdims=True)
+    place_of = lax.rem(iota((E, E), 1), PACK).astype(F32)
+    compact = ones_where(rank_col == place_of).astype(BF)
+    compact_ref[0:E] = compact
+    compact_ref[E : 2 * E] = compact
+    source = iota((E, E), 0)
+    for h in range(2):
+        wide = ones_where(rank_row == (source - h * PACK).astype(F32)).astype(BF)
+        widen_ref[0:E, cols(h)] = wide
+        widen_ref[E : 2 * E, cols(h)] = wide
     backward = jnp.concatenate([stiff_ref[d].T for d in range(3)], axis=0)
     node, entry = iota((FACE_PAD, FACE_MODES), 1), iota((FACE_PAD, FACE_MODES), 0)
     chosen = entry < 0
@@ -235,23 +264,74 @@
     lane = iota((1, E), 1)
     lane_group = lane // HALO
 
-    def taylor_rest(first_only):
+    def first_stack():
         for k in range(ORDER - 2):
             for group in GROUPS:
                 for g, t in zip(group, star(group, k % 2)):
                     split_into(t, g)
                     first_ref[g] += half[k + 1] * t
-                    if not first_only:
-                        second_ref[g] += rest[k + 1] * t
+                    second_ref[g] += rest[k + 1] * t
                 multiply(a_ref, 3 * MODES, group, (k + 1) % 2)
         for group in GROUPS:
             for g, t in zip(group, star(group, 0)):
-                value = first_ref[g] + half[5] * t
-                if first_only:
-                    value = jnp.where(small, value, second_ref[g])
-                else:
-                    second_ref[g] += rest[5] * t
-                first_ref[g] = value
+                first_ref[g] += half[5] * t
+                second_ref[g] += rest[5] * t
+
+    lower = lane < PACK
+
+    def sides(block):
+        high, low = high_low(block)
+        return jnp.concatenate([high.astype(BF), low.astype(BF)], axis=1)
+
+    def pack_star():
+        rows = FIELDS * 3 * 8
+        for p, pair in enumerate(PAIRS):
+            taken = [
+                dot(sides(star8_ref[f].reshape(rows, E)), compact_ref[...]) for f in pair
+            ]
+            both = jnp.where(lower, taken[0], taken[1] if len(pair) == 2 else 0.0)
+            packed_star_ref[p] = both.reshape(FIELDS, 3, 8, E)
+
+    def packed_star(pairs, slot):
+        fields = [g for p in pairs for g in PAIRS[p]]
+        totals = dict.fromkeys(fields)
+        for d in range(3):
+            for q in range(len(PAIRS)):
+                y = y_ref[slot, d * MODES : (d + 1) * MODES, cols(q)]
+                for g in fields:
+                    term = spread_mul(packed_star_ref[q, g, d], y)
+                    totals[g] = term if totals[g] is None else totals[g] + term
+        folded = []
+        for p in pairs:
+            one = totals[PAIRS[p][0]]
+            if len(PAIRS[p]) == 2:
+                two = totals[PAIRS[p][1]]
+                folded.append(
+                    jnp.where(lower, one, two) + pltpu.roll(jnp.where(lower, two, one), PACK, 1)
+                )
+            else:
+                folded.append(jnp.where(lower, one + pltpu.roll(one, PACK, 1), 0.0))
+        return folded
+
+    def second_stack():
+        for group in PAIR_GROUPS:
+            for p in group:
+                taken = [dot(sides(base_ref[f]), compact_ref[...]) for f in PAIRS[p]]
+                u = jnp.where(lower, taken[0], taken[1] if len(taken) == 2 else 0.0)
+                split_into(u, p)
+                j_ref[p] = half[0] * u
+            multiply(a_ref, 3 * MODES, group, 0)
+        for k in range(ORDER - 2):
+            for group in PAIR_GROUPS:
+                for p, t in zip(group, packed_star(group, k % 2)):
+                    split_into(t, p)
+                    j_ref[p] += half[k + 1] * t
+                multiply(a_ref, 3 * MODES, group, (k + 1) % 2)
+        for group in PAIR_GROUPS:
+            for p, t in zip(group, packed_star(group, 0)):
+                wide = dot(sides(j_ref[p] + half[5] * t), widen_ref[...])
+                for n, f in enumerate(PAIRS[p]):
+                    first_ref[f] = jnp.where(small, wide[:, cols(n)], second_ref[f])
 
     def exchange(phase):
         copies = []
@@ -397,27 +477,20 @@
             both[0:MODES, cols(n)] + both[MODES : 2 * MODES, cols(n)] for n in range(len(group))
         ]
 
-    taylor_rest(False)
+    first_stack()
     copies = exchange(0)
     for n in (2, 3, 11):
         loads[n].wait()
     for f in range(FIELDS):
         base_ref[f] = sol_ref[f]
+    pack_star()
     local_part()
     remote_part(0, copies)
     for group in GROUPS:
         update = lifted(group)
         for n, g in enumerate(group):
-            stepped = base_ref[g] - update[n]
-            base_ref[g] = stepped
-            prev_ref[g] = jnp.where(small, stepped, sol_ref[g])
-    for group in GROUPS:
-        for f in group:
-            u = prev_ref[f]
-            split_into(u, f)
-            first_ref[f] = half[0] * u
-        multiply(a_ref, 3 * MODES, group, 0)
-    taylor_rest(True)
+            base_ref[g] -= update[n]
+    second_stack()
     copies = exchange(1)
     local_part()
     remote_part(1, copies)
@@ -462,7 +535,7 @@
     field_block = pltpu.VMEM((FIELDS, MODES, E), F32)
     step = pl.pallas_call(
         functools.partial(kernel, n_dom, n_near),
-        out_shape=jax.ShapeDtypeStruct((FIELDS, MODES, E), F32),
+        out_shape=pltpu.VMEM((FIELDS, MODES, E), F32),
         in_specs=[pl.BlockSpec(memory_space=pltpu.HBM)] * 13,
         out_specs=pl.BlockSpec(memory_space=pltpu.VMEM),
         scratch_shapes=[pltpu.VMEM(value.shape, value.dtype) for value in operands]
@@ -474,7 +547,6 @@
             field_block,
             pltpu.VMEM((FACES, COLS), F32),
             pltpu.VMEM((FIELDS * FACE_PAD, 4 * E), F32),
-            field_block,
             pltpu.VMEM((3 * MODES, 3 * KPAD), BF),
             pltpu.VMEM((FACES + 3 * MODES, 3 * KPAD), BF),
             pltpu.VMEM((FACES, 3 * KPAD), BF),
@@ -487,6 +559,11 @@
             pltpu.SemaphoreType.DMA((2, 4)),
             pltpu.SemaphoreType.DMA((2, 4)),
             pltpu.SemaphoreType.DMA((13,)),
+            pltpu.VMEM((FIELDS, FIELDS, 3, 8, E), F32),
+            pltpu.VMEM((len(PAIRS), FIELDS, 3, 8, E), F32),
+            pltpu.VMEM((2 * E, E), BF),
+            pltpu.VMEM((2 * E, 2 * E), BF),
+            pltpu.VMEM((len(PAIRS), MODES, E), F32),
         ],
         compiler_params=pltpu.CompilerParams(
             collective_id=0, has_side_effects=True, vmem_limit_bytes=60 * 2**20

time: 29.1 us -> 26.2 us (0.900)
  Pallas kernels: 27.3 us -> 25.4 us
  local copies, waits for them, and re-layouts: 1.66 us -> 0.7 us
    pallas_call x1, Pallas kernels: 27.3 us -> 25.4 us  [on_device(): out = step(*operands)]
    unnamed x1, local copies, waits for them, and re-layouts: 1.66 us -> 0.7 us
where the time goes in v2:
time: 26.2 us; the launch traced here: 26.1 us
  Pallas kernels  25.4 us (97%)
  local copies, waits for them, and re-layouts  0.7 us (3%)
    pallas_call x1, Pallas kernels, on_device(): out = step(*operands)  25.4 us
    unnamed x1, local copies, waits for them, and re-layouts  0.7 us

profile of v2, /device:TPU:7, one launch (start us, length us, event | category | flops | bytes accessed | tf_op | source)
XLA Modules:
  0.0 26.1 jit_solution(3567096290022965692)
XLA Ops:
  0.0 25.4 %cluster_step.1 = f32[9,56,128]{2,1,0:T(8,128)S(1)} custom-call(f32[9,56,128]{2,1,0:T(8,128)} %bitcast.9, f32[9,9,3,128]{3,2,1,0:T(4,128)} %bitcast.10, f32[9,9,4,128]{3,2,1,0:T(4,128)} %bitcast.11, f32[9,9,4,128]{3,2,1,0:T(4,128)} %bitcast.12, f32[3,56,56]{2,1,0:T(8,128)} %refs_4_.1, f32[21,4,56]{2,1,0:T(4,128)} %bitcast.13, f32[21,4,56]{2,1,0:T(4,128)} %bitcast.14, ...), custom_call_target="tpu_custom_call" | custom-call | tf_op jit(solution)/shard_map/cluster_step/pallas_call | solution.py:573
  25.4 0.7 %copy.15 = f32[56,9,128]{2,0,1:T(8,128)} copy(f32[56,9,128]{2,0,1:T(8,128)S(1)} %bitcast.8) | data formatting | bytes 516096

commit v3 on v2

--- a/solution.py
+++ b/solution.py
@@ -202,56 +202,12 @@
             second_ref[f] = rest[0] * u
         multiply(a_ref, 3 * MODES, group, 0)
 
-    for n in (1, 12, 7, 8, 9, 10, 5, 6):
+    for n in (1, 12):
         loads[n].wait()
-    small = cluster_ref[...] == 0
     for f in range(FIELDS):
         for g in range(FIELDS):
             for d in range(3):
                 star8_ref[f, g, d] = jnp.broadcast_to(star_ref[f, g, d : d + 1, :], (8, E))
-    before = ones_where(iota((E, E), 0) < iota((E, E), 1)).astype(BF)
-    small_row = ones_where(small)
-    rank_row = dot(jnp.broadcast_to(small_row, (8, E)).astype(BF), before)[0:1]
-    rank_row = jnp.where(small, rank_row, -1.0)
-    square = iota((E, E), 0) == iota((E, E), 1)
-    rank_col = jnp.sum(jnp.where(square, rank_row, 0.0), axis=1, keepdims=True)
-    place_of = lax.rem(iota((E, E), 1), PACK).astype(F32)
-    compact = ones_where(rank_col == place_of).astype(BF)
-    compact_ref[0:E] = compact
-    compact_ref[E : 2 * E] = compact
-    source = iota((E, E), 0)
-    for h in range(2):
-        wide = ones_where(rank_row == (source - h * PACK).astype(F32)).astype(BF)
-        widen_ref[0:E, cols(h)] = wide
-        widen_ref[E : 2 * E, cols(h)] = wide
-    backward = jnp.concatenate([stiff_ref[d].T for d in range(3)], axis=0)
-    node, entry = iota((FACE_PAD, FACE_MODES), 1), iota((FACE_PAD, FACE_MODES), 0)
-    chosen = entry < 0
-    for spot, number in enumerate(ORDERED):
-        if number >= 0:
-            chosen = chosen | ((entry == spot) & (node == number))
-    chosen = ones_where(chosen)
-    project = jnp.concatenate([place_left(chosen, proj_ref[:, j, :]) for j in range(4)], axis=0)
-    lifts = jnp.concatenate([place_left(chosen, lift_ref[:, j, :]) for j in range(4)], axis=0)
-    b_ref[...] = threefold(jnp.concatenate([project, backward], axis=0))
-    p_ref[...] = threefold(project)
-    lift_high, lift_low = high_low(lifts.T)
-    row, col = iota((FACES, 2 * FACES), 0), iota((FACES, 2 * FACES), 1)
-    twice = ones_where((col == row) | (col == row + FACES)).astype(BF)
-    once = ones_where(col == row).astype(BF)
-    l_ref[...] = jnp.concatenate(
-        [dot(lift_high.astype(BF), twice), dot(lift_low.astype(BF), once)], axis=0
-    ).astype(BF)
-
-    part, slot_of = part_ref[...], slot_ref[...]
-    face_of = nface_ref[...]
-    local_key = jnp.where(part == 0, face_of * E + slot_of, -1)
-    remote_key = jnp.where(part > 0, face_of * (4 * HALO) + (part - 1) * HALO + slot_of, -1)
-    for i in range(4):
-        ohl_ref[:, cols(i)] = ones_where(local_key[i : i + 1, :] == iota((4 * E, E), 0)).astype(BF)
-        ohr_ref[:, cols(i)] = ones_where(
-            remote_key[i : i + 1, :] == iota((16 * HALO, E), 0)
-        ).astype(BF)
     spread = ones_where(iota((HALO, E), 0) == lax.rem(iota((HALO, E), 1), HALO)).astype(BF)
     sent = dot(halo_ref[...].astype(F32).astype(BF), spread)
     for r in range(4):
@@ -276,6 +232,51 @@
             for g, t in zip(group, star(group, 0)):
                 first_ref[g] += half[5] * t
                 second_ref[g] += rest[5] * t
+
+    def other_operators(small):
+        backward = jnp.concatenate([stiff_ref[d].T for d in range(3)], axis=0)
+        node, entry = iota((FACE_PAD, FACE_MODES), 1), iota((FACE_PAD, FACE_MODES), 0)
+        chosen = entry < 0
+        for spot, number in enumerate(ORDERED):
+            if number >= 0:
+                chosen = chosen | ((entry == spot) & (node == number))
+        chosen = ones_where(chosen)
+        project = jnp.concatenate([place_left(chosen, proj_ref[:, j, :]) for j in range(4)], axis=0)
+        lifts = jnp.concatenate([place_left(chosen, lift_ref[:, j, :]) for j in range(4)], axis=0)
+        b_ref[...] = threefold(jnp.concatenate([project, backward], axis=0))
+        p_ref[...] = threefold(project)
+        lift_high, lift_low = high_low(lifts.T)
+        row, col = iota((FACES, 2 * FACES), 0), iota((FACES, 2 * FACES), 1)
+        twice = ones_where((col == row) | (col == row + FACES)).astype(BF)
+        once = ones_where(col == row).astype(BF)
+        l_ref[...] = jnp.concatenate(
+            [dot(lift_high.astype(BF), twice), dot(lift_low.astype(BF), once)], axis=0
+        ).astype(BF)
+
+        part, slot_of = part_ref[...], slot_ref[...]
+        face_of = nface_ref[...]
+        local_key = jnp.where(part == 0, face_of * E + slot_of, -1)
+        remote_key = jnp.where(part > 0, face_of * (4 * HALO) + (part - 1) * HALO + slot_of, -1)
+        for i in range(4):
+            ohl_ref[:, cols(i)] = ones_where(local_key[i : i + 1, :] == iota((4 * E, E), 0)).astype(BF)
+            ohr_ref[:, cols(i)] = ones_where(
+                remote_key[i : i + 1, :] == iota((16 * HALO, E), 0)
+            ).astype(BF)
+        before = ones_where(iota((E, E), 0) < iota((E, E), 1)).astype(BF)
+        small_row = ones_where(small)
+        rank_row = dot(jnp.broadcast_to(small_row, (8, E)).astype(BF), before)[0:1]
+        rank_row = jnp.where(small, rank_row, -1.0)
+        square = iota((E, E), 0) == iota((E, E), 1)
+        rank_col = jnp.sum(jnp.where(square, rank_row, 0.0), axis=1, keepdims=True)
+        place_of = lax.rem(iota((E, E), 1), PACK).astype(F32)
+        compact = ones_where(rank_col == place_of).astype(BF)
+        compact_ref[0:E] = compact
+        compact_ref[E : 2 * E] = compact
+        source = iota((E, E), 0)
+        for h in range(2):
+            wide = ones_where(rank_row == (source - h * PACK).astype(F32)).astype(BF)
+            widen_ref[0:E, cols(h)] = wide
+            widen_ref[E : 2 * E, cols(h)] = wide
 
     lower = lane < PACK
 
@@ -347,30 +348,31 @@
             ],
             axis=1,
         )
-        taken = dot(stacked, ohs_ref[...])
-        for r in range(4):
-            block = taken[:, cols(r)]
-            packed = block[0:MODES]
-            for f in range(1, 8):
-                packed = jnp.where(lane_group == f, block[f * MODES : (f + 1) * MODES], packed)
-            tail = block[8 * MODES : 8 * MODES + 8]
-            for k in range(1, 7):
-                start = 8 * MODES + 8 * k
-                tail = jnp.where(lane_group == k, block[start : start + 8], tail)
-            send_buf[phase, r] = jnp.concatenate([packed, tail], axis=0)
-        if phase == 0:
-            pl.semaphore_wait(barrier, 4)
-        for r in range(4):
-            copy = pltpu.make_async_remote_copy(
-                src_ref=send_buf.at[phase, r],
-                dst_ref=recv_buf.at[phase, r],
-                send_sem=send_sem.at[phase, r],
-                recv_sem=recv_sem.at[phase, r],
-                device_id=targets[r],
-                device_id_type=MESH,
-            )
-            copy.start()
-            copies.append(copy)
+        for pair in ((2, 3), (0, 1)):
+            taken = dot(stacked, ohs_ref[:, cols(pair[0], 2)])
+            for n, r in enumerate(pair):
+                block = taken[:, cols(n)]
+                packed = block[0:MODES]
+                for f in range(1, 8):
+                    packed = jnp.where(lane_group == f, block[f * MODES : (f + 1) * MODES], packed)
+                tail = block[8 * MODES : 8 * MODES + 8]
+                for k in range(1, 7):
+                    start = 8 * MODES + 8 * k
+                    tail = jnp.where(lane_group == k, block[start : start + 8], tail)
+                send_buf[phase, r] = jnp.concatenate([packed, tail], axis=0)
+            if phase == 0 and pair[0] == 2:
+                pl.semaphore_wait(barrier, 4)
+            for r in pair:
+                copy = pltpu.make_async_remote_copy(
+                    src_ref=send_buf.at[phase, r],
+                    dst_ref=recv_buf.at[phase, r],
+                    send_sem=send_sem.at[phase, r],
+                    recv_sem=recv_sem.at[phase, r],
+                    device_id=targets[r],
+                    device_id_type=MESH,
+                )
+                copy.start()
+                copies.append(copy)
         return copies
 
     def gather(blocks, marks):
@@ -479,8 +481,10 @@
 
     first_stack()
     copies = exchange(0)
-    for n in (2, 3, 11):
+    for n in (7, 8, 9, 10, 5, 6, 2, 3, 11):
         loads[n].wait()
+    small = cluster_ref[...] == 0
+    other_operators(small)
     for f in range(FIELDS):
         base_ref[f] = sol_ref[f]
     pack_star()

time: 26.2 us -> 25.7 us (0.981)
  Pallas kernels: 25.4 us -> 24.9 us
    pallas_call x1, Pallas kernels: 25.4 us -> 24.9 us  [on_device(): out = step(*operands)]
where the time goes in v3:
time: 25.7 us; the launch traced here: 25.6 us
  Pallas kernels  24.9 us (97%)
  local copies, waits for them, and re-layouts  0.7 us (3%)
    pallas_call x1, Pallas kernels, on_device(): out = step(*operands)  24.9 us
    unnamed x1, local copies, waits for them, and re-layouts  0.7 us

profile of v3, /device:TPU:7, one launch (start us, length us, event | category | flops | bytes accessed | tf_op | source)
XLA Modules:
  0.0 25.6 jit_solution(14356272381981347162)
XLA Ops:
  0.0 24.9 %cluster_step.1 = f32[9,56,128]{2,1,0:T(8,128)S(1)} custom-call(f32[9,56,128]{2,1,0:T(8,128)} %bitcast.9, f32[9,9,3,128]{3,2,1,0:T(4,128)} %bitcast.10, f32[9,9,4,128]{3,2,1,0:T(4,128)} %bitcast.11, f32[9,9,4,128]{3,2,1,0:T(4,128)} %bitcast.12, f32[3,56,56]{2,1,0:T(8,128)} %refs_4_.1, f32[21,4,56]{2,1,0:T(4,128)} %bitcast.13, f32[21,4,56]{2,1,0:T(4,128)} %bitcast.14, ...), custom_call_target="tpu_custom_call" | custom-call | tf_op jit(solution)/shard_map/cluster_step/pallas_call | solution.py:577
  24.9 0.7 %copy.15 = f32[56,9,128]{2,0,1:T(8,128)} copy(f32[56,9,128]{2,0,1:T(8,128)S(1)} %bitcast.8) | data formatting | bytes 516096

commit v4 on v3

--- a/solution.py
+++ b/solution.py
@@ -116,7 +116,6 @@
         halo_ref,
     ) = held
     (
-        r_ref,
         y_ref,
         first_ref,
         second_ref,
@@ -165,18 +164,18 @@
     stiff = jnp.concatenate([stiff_ref[d] for d in range(3)], axis=0)
     a_ref[...] = threefold(stiff)
 
+    held_parts = {}
+
     def split_into(t, f):
         high, low = high_low(t)
         zero = jnp.zeros((KPAD - MODES, E), F32)
         high = jnp.concatenate([high, zero], axis=0).astype(BF)
         low = jnp.concatenate([low, zero], axis=0).astype(BF)
-        r_ref[0:KPAD, cols(f)] = high
-        r_ref[KPAD : 2 * KPAD, cols(f)] = low
-        r_ref[2 * KPAD : 3 * KPAD, cols(f)] = high
+        held_parts[f] = jnp.concatenate([high, low, high], axis=0)
 
     def multiply(matrix, rows, group, slot):
-        span = cols(group[0], len(group))
-        y_ref[slot, 0:rows, span] = dot(matrix[...], r_ref[:, span])
+        columns = jnp.concatenate([held_parts[f] for f in group], axis=1)
+        y_ref[slot, 0:rows, cols(group[0], len(group))] = dot(matrix[...], columns)
 
     def spread_mul(tile, y):
         return (tile[None] * y.reshape(MODES // 8, 8, E)).reshape(MODES, E)
@@ -451,11 +450,10 @@
         for i in range(4):
             turn = turn_ref[i : i + 1, :]
             for_one, for_two = turn == 1, turn == 2
-            totals = [x_ref[i * FACE_PAD : (i + 1) * FACE_PAD, cols(g)] for g in range(FIELDS)]
             for f in range(FIELDS):
                 raw = g_ref[f * FACE_PAD : (f + 1) * FACE_PAD, cols(i)]
                 v = [raw[c * 8 : (c + 1) * 8] for c in range(3)]
-                y = jnp.concatenate(
+                g_ref[f * FACE_PAD : (f + 1) * FACE_PAD, cols(i)] = jnp.concatenate(
                     [
                         jnp.where(
                             for_one, v[(c + 1) % 3], jnp.where(for_two, v[(c + 2) % 3], v[c])
@@ -464,17 +462,24 @@
                     ],
                     axis=0,
                 )
-                for g in range(FIELDS):
-                    totals[g] = totals[g] + minus_ref[f, g, i : i + 1, :] * y
-            for g in range(FIELDS):
-                x_ref[i * FACE_PAD : (i + 1) * FACE_PAD, cols(g)] = totals[g]
+
+    def outside(group):
+        totals = [
+            [x_ref[i * FACE_PAD : (i + 1) * FACE_PAD, cols(g)] for i in range(4)] for g in group
+        ]
+        for f in range(FIELDS):
+            for i in range(4):
+                y = g_ref[f * FACE_PAD : (f + 1) * FACE_PAD, cols(i)]
+                for n, g in enumerate(group):
+                    totals[n][i] = totals[n][i] + minus_ref[f, g, i : i + 1, :] * y
+        return [jnp.concatenate(total, axis=0) for total in totals]
 
     def lifted(group):
-        for g in group:
-            high, low = high_low(x_ref[:, cols(g)])
-            r_ref[0:FACES, cols(g)] = high.astype(BF)
-            r_ref[FACES : 2 * FACES, cols(g)] = low.astype(BF)
-        both = dot(l_ref[...], r_ref[:, cols(group[0], len(group))])
+        parts = []
+        for g, flux in zip(group, outside(group)):
+            high, low = high_low(flux)
+            parts.append(jnp.concatenate([high.astype(BF), low.astype(BF)], axis=0))
+        both = dot(l_ref[...], jnp.concatenate(parts, axis=1))
         return [
             both[0:MODES, cols(n)] + both[MODES : 2 * MODES, cols(n)] for n in range(len(group))
         ]
@@ -544,7 +549,6 @@
         out_specs=pl.BlockSpec(memory_space=pltpu.VMEM),
         scratch_shapes=[pltpu.VMEM(value.shape, value.dtype) for value in operands]
         + [
-            pltpu.VMEM((3 * KPAD, COLS), BF),
             pltpu.VMEM((2, FACES + 3 * MODES, COLS), F32),
             field_block,
             field_block,

time: 25.7 us -> 24.9 us (0.969)
  Pallas kernels: 24.9 us -> 24.1 us
    pallas_call x1, Pallas kernels: 24.9 us -> 24.1 us  [on_device(): out = step(*operands)]
where the time goes in v4:
time: 24.9 us; the launch traced here: 24.8 us
  Pallas kernels  24.1 us (97%)
  local copies, waits for them, and re-layouts  0.7 us (3%)
    pallas_call x1, Pallas kernels, on_device(): out = step(*operands)  24.1 us
    unnamed x1, local copies, waits for them, and re-layouts  0.7 us

profile of v4, /device:TPU:7, one launch (start us, length us, event | category | flops | bytes accessed | tf_op | source)
XLA Modules:
  0.0 24.8 jit_solution(17184078150319419688)
XLA Ops:
  0.0 24.1 %cluster_step.1 = f32[9,56,128]{2,1,0:T(8,128)S(1)} custom-call(f32[9,56,128]{2,1,0:T(8,128)} %bitcast.9, f32[9,9,3,128]{3,2,1,0:T(4,128)} %bitcast.10, f32[9,9,4,128]{3,2,1,0:T(4,128)} %bitcast.11, f32[9,9,4,128]{3,2,1,0:T(4,128)} %bitcast.12, f32[3,56,56]{2,1,0:T(8,128)} %refs_4_.1, f32[21,4,56]{2,1,0:T(4,128)} %bitcast.13, f32[21,4,56]{2,1,0:T(4,128)} %bitcast.14, ...), custom_call_target="tpu_custom_call" | custom-call | tf_op jit(solution)/shard_map/cluster_step/pallas_call | solution.py:581
  24.1 0.7 %copy.15 = f32[56,9,128]{2,0,1:T(8,128)} copy(f32[56,9,128]{2,0,1:T(8,128)S(1)} %bitcast.8) | data formatting | bytes 516096

commit v5 on v4

--- a/solution.py
+++ b/solution.py
@@ -139,6 +139,9 @@
         compact_ref,
         widen_ref,
         j_ref,
+        pick_ref,
+        slot_ints,
+        minus8_ref,
     ) = refs[27:]
     loads = [
         pltpu.make_async_copy(source, target, load_sem.at[n])
@@ -255,12 +258,37 @@
         part, slot_of = part_ref[...], slot_ref[...]
         face_of = nface_ref[...]
         local_key = jnp.where(part == 0, face_of * E + slot_of, -1)
-        remote_key = jnp.where(part > 0, face_of * (4 * HALO) + (part - 1) * HALO + slot_of, -1)
+        slot_key = jnp.where(part > 0, (part - 1) * HALO + slot_of, -1).astype(F32)
+        diagonal = iota((E, E), 0) == iota((E, E), 1)
+        slot_lane = lax.rem(iota((E, E), 1), PACK).astype(F32)
         for i in range(4):
             ohl_ref[:, cols(i)] = ones_where(local_key[i : i + 1, :] == iota((4 * E, E), 0)).astype(BF)
-            ohr_ref[:, cols(i)] = ones_where(
-                remote_key[i : i + 1, :] == iota((16 * HALO, E), 0)
-            ).astype(BF)
+            key = slot_key[i : i + 1, :]
+            scatter = ones_where(key == iota((E, E), 0).astype(F32)).astype(BF)
+            ohr_ref[0:E, cols(i)] = scatter
+            ohr_ref[E : 2 * E, cols(i)] = scatter
+            key_col = jnp.sum(jnp.where(diagonal, key, 0.0), axis=1, keepdims=True)
+            pick_ref[i * E : (i + 1) * E, :] = ones_where(key_col == slot_lane).astype(BF)
+        for n, table in enumerate((face_of, turn_ref[...])):
+            line = jnp.concatenate([table[i : i + 1, :] for i in range(4)], axis=1).astype(F32)
+            slot_ints[n] = dot(jnp.broadcast_to(line, (8, 4 * E)).astype(BF), pick_ref[...])
+        for f in range(FIELDS):
+            line = jnp.concatenate(
+                [
+                    jnp.concatenate(
+                        [
+                            jnp.broadcast_to(minus_ref[f, g, i : i + 1, :], (8, E))
+                            for g in range(FIELDS)
+                        ],
+                        axis=0,
+                    )
+                    for i in range(4)
+                ],
+                axis=1,
+            )
+            high, low = high_low(line)
+            both = dot(high.astype(BF), pick_ref[...]) + dot(low.astype(BF), pick_ref[...])
+            minus8_ref[f] = both.reshape(FIELDS, 8, E)
         before = ones_where(iota((E, E), 0) < iota((E, E), 1)).astype(BF)
         small_row = ones_where(small)
         rank_row = dot(jnp.broadcast_to(small_row, (8, E)).astype(BF), before)[0:1]
@@ -316,7 +344,11 @@
     def second_stack():
         for group in PAIR_GROUPS:
             for p in group:
-                taken = [dot(sides(base_ref[f]), compact_ref[...]) for f in PAIRS[p]]
+                taken = dot(
+                    sides(jnp.concatenate([base_ref[f] for f in PAIRS[p]], axis=0)),
+                    compact_ref[...],
+                )
+                taken = [taken[n * MODES : (n + 1) * MODES] for n in range(len(PAIRS[p]))]
                 u = jnp.where(lower, taken[0], taken[1] if len(taken) == 2 else 0.0)
                 split_into(u, p)
                 j_ref[p] = half[0] * u
@@ -375,16 +407,26 @@
         return copies
 
     def gather(blocks, marks):
-        sides = []
+        tall = []
         for block in blocks:
             high, low = high_low(block)
-            sides.append(jnp.concatenate([high, low], axis=0).astype(BF))
-        both = dot(jnp.concatenate(sides, axis=1), marks[...])
+            tall.append(jnp.concatenate([high, low], axis=0).astype(BF))
+        both = dot(jnp.concatenate(tall, axis=1), marks[...])
         rows = FIELDS * FACE_PAD
         return both[0:rows] + both[rows : 2 * rows]
 
     def by_field(read):
         return jnp.concatenate([read(f) for f in range(FIELDS)], axis=0)
+
+    def rotated(raw, for_one, for_two):
+        v = [raw[c * 8 : (c + 1) * 8] for c in range(3)]
+        return jnp.concatenate(
+            [
+                jnp.where(for_one, v[(c + 1) % 3], jnp.where(for_two, v[(c + 2) % 3], v[c]))
+                for c in range(3)
+            ],
+            axis=0,
+        )
 
     def local_part():
         for group in GROUPS:
@@ -400,10 +442,12 @@
         )
         for i in range(4):
             totals = [None] * FIELDS
+            turn = turn_ref[i : i + 1, :]
             for f in range(FIELDS):
                 y = y_ref[0, i * FACE_PAD : (i + 1) * FACE_PAD, cols(f)]
+                z = rotated(g_ref[f * FACE_PAD : (f + 1) * FACE_PAD, cols(i)], turn == 1, turn == 2)
                 for g in range(FIELDS):
-                    term = plus_ref[f, g, i : i + 1, :] * y
+                    term = plus_ref[f, g, i : i + 1, :] * y + minus_ref[f, g, i : i + 1, :] * z
                     totals[g] = term if totals[g] is None else totals[g] + term
             for g in range(FIELDS):
                 x_ref[i * FACE_PAD : (i + 1) * FACE_PAD, cols(g)] = totals[g]
@@ -438,41 +482,27 @@
                     split_into(jnp.concatenate(tiles, axis=0), f)
             multiply(p_ref, FACES, group, 1)
 
-        def pair(j):
-            def read(f):
-                low = y_ref[1, j * FACE_PAD : (j + 1) * FACE_PAD, cols(f)]
-                high = y_ref[1, (j + 1) * FACE_PAD : (j + 2) * FACE_PAD, cols(f)]
-                return jnp.where(lane < E // 2, low, high)
-
-            return by_field(read)
-
-        g_ref[...] += gather([pair(0), pair(2)], ohr_ref)
-        for i in range(4):
-            turn = turn_ref[i : i + 1, :]
-            for_one, for_two = turn == 1, turn == 2
-            for f in range(FIELDS):
-                raw = g_ref[f * FACE_PAD : (f + 1) * FACE_PAD, cols(i)]
-                v = [raw[c * 8 : (c + 1) * 8] for c in range(3)]
-                g_ref[f * FACE_PAD : (f + 1) * FACE_PAD, cols(i)] = jnp.concatenate(
-                    [
-                        jnp.where(
-                            for_one, v[(c + 1) % 3], jnp.where(for_two, v[(c + 2) % 3], v[c])
-                        )
-                        for c in range(3)
-                    ],
-                    axis=0,
-                )
+        face, turn = slot_ints[0, 0:1, :], slot_ints[1, 0:1, :]
+        totals = [None] * FIELDS
+        for f in range(FIELDS):
+            t = [y_ref[1, j * FACE_PAD : (j + 1) * FACE_PAD, cols(f)] for j in range(4)]
+            own = jnp.where(
+                face == 0.0, t[0], jnp.where(face == 1.0, t[1], jnp.where(face == 2.0, t[2], t[3]))
+            )
+            y = rotated(own, turn == 1.0, turn == 2.0)
+            for g in range(FIELDS):
+                term = (minus8_ref[f, g][None] * y.reshape(3, 8, E)).reshape(FACE_PAD, E)
+                totals[g] = term if totals[g] is None else totals[g] + term
+        g_ref[...] = dot(sides(jnp.concatenate(totals, axis=0)), ohr_ref[...])
 
     def outside(group):
-        totals = [
-            [x_ref[i * FACE_PAD : (i + 1) * FACE_PAD, cols(g)] for i in range(4)] for g in group
+        return [
+            x_ref[:, cols(g)]
+            + jnp.concatenate(
+                [g_ref[g * FACE_PAD : (g + 1) * FACE_PAD, cols(i)] for i in range(4)], axis=0
+            )
+            for g in group
         ]
-        for f in range(FIELDS):
-            for i in range(4):
-                y = g_ref[f * FACE_PAD : (f + 1) * FACE_PAD, cols(i)]
-                for n, g in enumerate(group):
-                    totals[n][i] = totals[n][i] + minus_ref[f, g, i : i + 1, :] * y
-        return [jnp.concatenate(total, axis=0) for total in totals]
 
     def lifted(group):
         parts = []
@@ -572,6 +602,9 @@
             pltpu.VMEM((2 * E, E), BF),
             pltpu.VMEM((2 * E, 2 * E), BF),
             pltpu.VMEM((len(PAIRS), MODES, E), F32),
+            pltpu.VMEM((4 * E, E), BF),
+            pltpu.VMEM((2, 8, E), F32),
+            pltpu.VMEM((FIELDS, FIELDS, 8, E), F32),
         ],
         compiler_params=pltpu.CompilerParams(
             collective_id=0, has_side_effects=True, vmem_limit_bytes=60 * 2**20

time: 24.9 us -> 24.3 us (0.976)
  Pallas kernels: 24.1 us -> 23.5 us
    pallas_call x1, Pallas kernels: 24.1 us -> 23.5 us  [on_device(): out = step(*operands)]
where the time goes in v5:
time: 24.3 us; the launch traced here: 24.2 us
  Pallas kernels  23.5 us (97%)
  local copies, waits for them, and re-layouts  0.7 us (3%)
    pallas_call x1, Pallas kernels, on_device(): out = step(*operands)  23.5 us
    unnamed x1, local copies, waits for them, and re-layouts  0.7 us

profile of v5, /device:TPU:7, one launch (start us, length us, event | category | flops | bytes accessed | tf_op | source)
XLA Modules:
  0.0 24.2 jit_solution(6532114778202373019)
XLA Ops:
  0.0 23.5 %cluster_step.1 = f32[9,56,128]{2,1,0:T(8,128)S(1)} custom-call(f32[9,56,128]{2,1,0:T(8,128)} %bitcast.9, f32[9,9,3,128]{3,2,1,0:T(4,128)} %bitcast.10, f32[9,9,4,128]{3,2,1,0:T(4,128)} %bitcast.11, f32[9,9,4,128]{3,2,1,0:T(4,128)} %bitcast.12, f32[3,56,56]{2,1,0:T(8,128)} %refs_4_.1, f32[21,4,56]{2,1,0:T(4,128)} %bitcast.13, f32[21,4,56]{2,1,0:T(4,128)} %bitcast.14, ...), custom_call_target="tpu_custom_call" | custom-call | tf_op jit(solution)/shard_map/cluster_step/pallas_call | solution.py:614
  23.5 0.7 %copy.15 = f32[56,9,128]{2,0,1:T(8,128)} copy(f32[56,9,128]{2,0,1:T(8,128)S(1)} %bitcast.8) | data formatting | bytes 516096

commit v6 on v5

--- a/solution.py
+++ b/solution.py
@@ -379,7 +379,7 @@
             ],
             axis=1,
         )
-        for pair in ((2, 3), (0, 1)):
+        for pair in ((0, 1), (2, 3)):
             taken = dot(stacked, ohs_ref[:, cols(pair[0], 2)])
             for n, r in enumerate(pair):
                 block = taken[:, cols(n)]
@@ -391,7 +391,7 @@
                     start = 8 * MODES + 8 * k
                     tail = jnp.where(lane_group == k, block[start : start + 8], tail)
                 send_buf[phase, r] = jnp.concatenate([packed, tail], axis=0)
-            if phase == 0 and pair[0] == 2:
+            if phase == 0 and pair[0] == 0:
                 pl.semaphore_wait(barrier, 4)
             for r in pair:
                 copy = pltpu.make_async_remote_copy(

time: 24.3 us -> 24.2 us (level)
  no operation moved by 1% of the time
where the time goes in v6:
time: 24.2 us; the launch traced here: 24.1 us
  Pallas kernels  23.4 us (97%)
  local copies, waits for them, and re-layouts  0.7 us (3%)
    pallas_call x1, Pallas kernels, on_device(): out = step(*operands)  23.4 us
    unnamed x1, local copies, waits for them, and re-layouts  0.7 us

profile of v6, /device:TPU:7, one launch (start us, length us, event | category | flops | bytes accessed | tf_op | source)
XLA Modules:
  0.0 24.1 jit_solution(3728540761328061040)
XLA Ops:
  0.0 23.4 %cluster_step.1 = f32[9,56,128]{2,1,0:T(8,128)S(1)} custom-call(f32[9,56,128]{2,1,0:T(8,128)} %bitcast.9, f32[9,9,3,128]{3,2,1,0:T(4,128)} %bitcast.10, f32[9,9,4,128]{3,2,1,0:T(4,128)} %bitcast.11, f32[9,9,4,128]{3,2,1,0:T(4,128)} %bitcast.12, f32[3,56,56]{2,1,0:T(8,128)} %refs_4_.1, f32[21,4,56]{2,1,0:T(4,128)} %bitcast.13, f32[21,4,56]{2,1,0:T(4,128)} %bitcast.14, ...), custom_call_target="tpu_custom_call" | custom-call | tf_op jit(solution)/shard_map/cluster_step/pallas_call | solution.py:614
  23.4 0.7 %copy.15 = f32[56,9,128]{2,0,1:T(8,128)} copy(f32[56,9,128]{2,0,1:T(8,128)S(1)} %bitcast.8) | data formatting | bytes 516096
